TPU v7x, 32 devices: a whole 2x2x4 slice. The times are simulated.
32 devices in a mesh: view: 4 (over y, x), brick: 8 (over z, core).
Axes of the slice: x: 2, y: 2, z: 4, core: 2. Of those that a mesh axis runs over, the one named last changes fastest.
Arguments:
- view_stacks: float32 [4, 128, 256, 256], P('view', 'brick'), may hold values from 0.2 to 5
- point_spread: float32 [4, 128, 256, 256], P('view', 'brick'), may hold values from 0 to 2, as said below
- weights_depth: float32 [4, 128, 128], P('view'), may hold values from 0 to 2, as said below
- weights_rows: float32 [4, 256, 256], P('view'), may hold values from 0 to 2, as said below
- weights_cols: float32 [4, 256, 256], P('view'), may hold values from 0 to 2, as said below
- depth_start: int32 [4, 256, 256], P('view'), may hold values from 0 to 63
- depth_stop: int32 [4, 256, 256], P('view'), may hold values from 65 to 128
Outputs:
- joined_brick: float32 [128, 256, 256], P('brick')
- deconvolved: float32 [128, 256, 256], P('brick')
Inputs may be any that keep to these rules, and one draw needn't show every extreme that they name: `point_spread`: nonnegative. `weights_depth`: nonnegative. `weights_rows`: nonnegative. `weights_cols`: nonnegative.
All inputs are finite; a program needn't handle non-finite values.
Results may differ from a plain program's by a relative error of at most 0.00012.
Values sent between devices are 32-bit elements; how exact they have to be, the bound alone decides.
A program may use at most 192 MiB of HBM per device.

v0:
```python
import math
import jax
import jax.numpy as jnp
from jax import lax
from jax.sharding import PartitionSpec as P

highest = lax.Precision.HIGHEST
einsum_forms = ("kyx,kj->jyx", "zkx,kj->zjx", "zyk,kj->zyj")


def dft_tables(length):
    counter = jnp.arange(length, dtype=jnp.int32)
    product = counter[:, None] * counter[None, :] % length
    angles = product.astype(jnp.float32) * (2.0 * math.pi / length)
    return (jnp.cos(angles), jnp.sin(angles))


def along_axis(values_in, table, axis_index):
    return jnp.einsum(einsum_forms[axis_index], values_in, table, precision=highest)


def forward_axis(real_part, imag_part, axis_index):
    cosine, sine = dft_tables(real_part.shape[axis_index])
    if imag_part is None:
        return (along_axis(real_part, cosine, axis_index), -along_axis(real_part, sine, axis_index))
    new_real = along_axis(real_part, cosine, axis_index) + along_axis(imag_part, sine, axis_index)
    new_imag = along_axis(imag_part, cosine, axis_index) - along_axis(real_part, sine, axis_index)
    return (new_real, new_imag)


def inverse_axis(real_part, imag_part, axis_index, real_only):
    length = real_part.shape[axis_index]
    cosine, sine = dft_tables(length)
    scale = 1.0 / length
    new_real = (
        along_axis(real_part, cosine, axis_index) - along_axis(imag_part, sine, axis_index)
    ) * scale
    if real_only:
        return new_real
    new_imag = (
        along_axis(imag_part, cosine, axis_index) + along_axis(real_part, sine, axis_index)
    ) * scale
    return (new_real, new_imag)


def resample_view(source, depth_map, row_map, col_map):
    across = jnp.einsum("zyx,ax->zya", source, col_map, precision=highest)
    across = jnp.einsum("zyx,by->zbx", across, row_map, precision=highest)
    mixed = jnp.einsum(
        "zyx,cz->cyx",
        lax.all_to_all(across, "brick", split_axis=1, concat_axis=0, tiled=True),
        depth_map,
        precision=highest,
    )
    return lax.all_to_all(mixed, "brick", split_axis=0, concat_axis=1, tiled=True)


def forward_transform(grid_values):
    real_part, imag_part = forward_axis(grid_values, None, 2)
    real_part, imag_part = forward_axis(real_part, imag_part, 1)
    depth_real, depth_imag = forward_axis(
        lax.all_to_all(real_part, "brick", split_axis=1, concat_axis=0, tiled=True),
        lax.all_to_all(imag_part, "brick", split_axis=1, concat_axis=0, tiled=True),
        0,
    )
    return (
        lax.all_to_all(depth_real, "brick", split_axis=0, concat_axis=1, tiled=True),
        lax.all_to_all(depth_imag, "brick", split_axis=0, concat_axis=1, tiled=True),
    )


def inverse_transform(real_part, imag_part):
    real_part, imag_part = (
        lax.all_to_all(real_part, "brick", split_axis=1, concat_axis=0, tiled=True),
        lax.all_to_all(imag_part, "brick", split_axis=1, concat_axis=0, tiled=True),
    )
    real_part, imag_part = inverse_axis(real_part, imag_part, 0, False)
    real_part, imag_part = inverse_axis(
        lax.all_to_all(real_part, "brick", split_axis=0, concat_axis=1, tiled=True),
        lax.all_to_all(imag_part, "brick", split_axis=0, concat_axis=1, tiled=True),
        1,
        False,
    )
    return inverse_axis(real_part, imag_part, 2, True)


def per_device(
    view_stacks, point_spread, weights_depth, weights_rows, weights_cols, depth_start, depth_stop
):
    resampled = resample_view(view_stacks[0], weights_depth[0], weights_rows[0], weights_cols[0])
    planes_here = resampled.shape[0]
    depth_index = lax.axis_index("brick") * planes_here + jnp.arange(planes_here, dtype=jnp.int32)
    depth_grid = depth_index[:, None, None]
    covered = jnp.logical_and(
        depth_grid >= depth_start[0][None], depth_grid < depth_stop[0][None]
    ).astype(jnp.float32)
    view_weight = 0.05 + covered * (1.0 + jnp.log(1.0 + resampled * resampled))
    weighted = view_weight * resampled
    total_signal, total_weight = lax.psum((weighted, view_weight), "view")
    joined_brick = total_signal / total_weight
    otf_real, otf_imag = forward_transform(point_spread[0])
    joined_real, joined_imag = forward_transform(joined_brick)
    blurred = inverse_transform(
        joined_real * otf_real - joined_imag * otf_imag,
        joined_real * otf_imag + joined_imag * otf_real,
    )
    ratio = resampled / blurred
    ratio_real, ratio_imag = forward_transform(ratio)
    correction = inverse_transform(
        ratio_real * otf_real + ratio_imag * otf_imag, ratio_imag * otf_real - ratio_real * otf_imag
    )
    correction_total = lax.psum(view_weight * correction, "view")
    deconvolved = joined_brick * correction_total / total_weight
    return (joined_brick, deconvolved)


def solution(mesh):
    return jax.shard_map(
        per_device,
        mesh=mesh,
        in_specs=(
            P("view", "brick", None, None),
            P("view", "brick", None, None),
            P("view", None, None),
            P("view", None, None),
            P("view", None, None),
            P("view", None, None),
            P("view", None, None),
        ),
        out_specs=(P("brick", None, None), P("brick", None, None)),
        check_vma=False,
    )
```

profile of v0, /device:TPU:0, one launch (start us, length us, event | category | flops | bytes accessed | tf_op | source)
XLA Modules:
  0.0 2484.0 jit_solution(6937730432940994262)
XLA Ops:
  8.1 5.7 fusion.25
  13.8 5.0 convolution_bitcast_fusion
  18.8 5.4 copy.144
  24.3 6.3 all-to-all-start
  30.6 10.7 fusion.16
  41.4 7.6 fusion.18
  49.0 8.1 fusion.10
  57.1 7.6 add_bitcast_fusion.1
  69.3 55.4 %all-to-all-done = f32[16,256,256]{2,0,1:T(8,128)} async-done(((f32[16,256,256]{2,0,1:T(8,128)}), f32[16,256,256]{2,0,1:T(8,128)}, u32[]{:S(2)}, u32[]{:S(2)}) %all-to-all-start) | async-done | bytes 4194336 | tf_op jit(solution)/shard_map/all_to_all | solution.py:51
  133.9 9.4 fusion.47
  143.3 5.4 copy.148
  148.7 74.5 %all-to-all-done.5 = f32[16,256,256]{2,0,1:T(8,128)} async-done(((f32[16,256,256]{2,0,1:T(8,128)}), f32[16,256,256]{2,0,1:T(8,128)}, u32[]{:S(2)}, u32[]{:S(2)}) %all-to-all-start.5) | async-done | bytes 4194336 | tf_op jit(solution)/shard_map/all_to_all | solution.py:62
  227.9 11.0 fusion.8
  238.9 7.6 subtract_bitcast_fusion.1
  251.0 70.8 %all-to-all-done.1 = f32[128,32,256]{2,1,0:T(8,128)} async-done(((f32[128,32,256]{2,1,0:T(8,128)}), f32[128,32,256]{2,1,0:T(8,128)}, u32[]{:S(2)}, u32[]{:S(2)}) %all-to-all-start.1) | async-done | bytes 4194336 | tf_op jit(solution)/shard_map/all_to_all | solution.py:55
  329.1 5.5 fusion.24
  334.6 4.9 copy.166
  339.5 80.9 %all-to-all-done.6 = f32[16,256,256]{2,0,1:T(8,128)} async-done(((f32[16,256,256]{2,0,1:T(8,128)}), f32[16,256,256]{2,0,1:T(8,128)}, u32[]{:S(2)}, u32[]{:S(2)}) %all-to-all-start.6) | async-done | bytes 4194336 | tf_op jit(solution)/shard_map/all_to_all | solution.py:63
  440.6 68.1 %all-reduce.6.cloned.1.call-done = (f32[16,256,256]{2,1,0:T(8,128)}, f32[16,256,256]{2,1,0:T(8,128)}) async-done(((f32[16,256,256]{2,1,0:T(8,128)}, f32[16,256,256]{2,1,0:T(8,128)}), (f32[16,256,256]{2,1,0:T(8,128)}, f32[16,256,256]{2,1,0:T(8,128)})) %all-reduce.6.cloned.1.call-update) | async-done | bytes 8388624 | tf_op jit(solution)/shard_map/psum | solution.py:99
  521.8 5.6 fusion.111
  527.4 4.9 add_bitcast_fusion.2
  541.6 7.5 fusion.87
  558.1 77.5 %all-to-all-done.2 = f32[16,256,256]{2,0,1:T(8,128)} async-done(((f32[16,256,256]{2,0,1:T(8,128)}), f32[16,256,256]{2,0,1:T(8,128)}, u32[]{:S(2)}, u32[]{:S(2)}) %all-to-all-start.2) | async-done | bytes 4194336 | tf_op jit(solution)/shard_map/all_to_all | solution.py:62
  640.4 6.0 fusion.185
  654.9 79.5 %all-to-all-done.3 = f32[16,256,256]{2,0,1:T(8,128)} async-done(((f32[16,256,256]{2,0,1:T(8,128)}), f32[16,256,256]{2,0,1:T(8,128)}, u32[]{:S(2)}, u32[]{:S(2)}) %all-to-all-start.3) | async-done | bytes 4194336 | tf_op jit(solution)/shard_map/all_to_all | solution.py:63
  734.4 5.0 all-to-all-start.7
  759.1 74.3 %all-to-all-done.7 = f32[128,32,256]{2,1,0:T(8,128)} async-done(((f32[128,32,256]{2,1,0:T(8,128)}), f32[128,32,256]{2,1,0:T(8,128)}, u32[]{:S(2)}, u32[]{:S(2)}) %all-to-all-start.7) | async-done | bytes 4194336 | tf_op jit(solution)/shard_map/all_to_all | solution.py:67
  838.1 6.0 fusion.187
  852.7 79.4 %all-to-all-done.8 = f32[128,32,256]{2,1,0:T(8,128)} async-done(((f32[128,32,256]{2,1,0:T(8,128)}), f32[128,32,256]{2,1,0:T(8,128)}, u32[]{:S(2)}, u32[]{:S(2)}) %all-to-all-start.8) | async-done | bytes 4194336 | tf_op jit(solution)/shard_map/all_to_all | solution.py:68
  932.1 97.9 %all_to_all.342 = f32[128,32,256]{2,1,0:T(8,128)S(1)} all-to-all(f32[128,32,256]{2,1,0:T(8,128)} %copy.158), channel_id=1, replica_groups=mesh['view'=4,'brick'=8] {'brick'}, dimensions={0} | all-to-all | bytes 8388608 | tf_op jit(solution)/shard_map/all_to_all | solution.py:67
  1030.0 10.5 multiply_subtract_fusion.1
  1059.1 87.0 %all-to-all-done.11 = f32[16,256,256]{2,0,1:T(8,128)} async-done(((f32[16,256,256]{2,0,1:T(8,128)}), f32[16,256,256]{2,0,1:T(8,128)}, u32[]{:S(2)}, u32[]{:S(2)}) %all-to-all-start.11) | async-done | bytes 4194336 | tf_op jit(solution)/shard_map/all_to_all | solution.py:75
  1146.0 5.0 all-to-all-start.10
  1155.8 89.2 %all-to-all-done.10 = f32[16,256,256]{2,0,1:T(8,128)} async-done(((f32[16,256,256]{2,0,1:T(8,128)}), f32[16,256,256]{2,0,1:T(8,128)}, u32[]{:S(2)}, u32[]{:S(2)}) %all-to-all-start.10) | async-done | bytes 4194336 | tf_op jit(solution)/shard_map/all_to_all | solution.py:74
  1266.1 6.0 fusion.179
  1280.8 79.3 %all-to-all-done.13 = f32[128,32,256]{2,1,0:T(8,128)} async-done(((f32[128,32,256]{2,1,0:T(8,128)}), f32[128,32,256]{2,1,0:T(8,128)}, u32[]{:S(2)}, u32[]{:S(2)}) %all-to-all-start.13) | async-done | bytes 4194336 | tf_op jit(solution)/shard_map/all_to_all | solution.py:80
  1367.1 7.1 fusion.99
  1374.2 7.5 fusion.82
  1381.7 76.9 %all-to-all-done.12 = f32[128,32,256]{2,1,0:T(8,128)} async-done(((f32[128,32,256]{2,1,0:T(8,128)}), f32[128,32,256]{2,1,0:T(8,128)}, u32[]{:S(2)}, u32[]{:S(2)}) %all-to-all-start.12) | async-done | bytes 4194336 | tf_op jit(solution)/shard_map/all_to_all | solution.py:79
  1465.9 5.1 fusion.113
  1475.9 5.0 bitcast_divide_fusion
  1508.9 7.5 fusion.77
  1525.6 77.4 %all-to-all-done.14 = f32[16,256,256]{2,0,1:T(8,128)} async-done(((f32[16,256,256]{2,0,1:T(8,128)}), f32[16,256,256]{2,0,1:T(8,128)}, u32[]{:S(2)}, u32[]{:S(2)}) %all-to-all-start.14) | async-done | bytes 4194336 | tf_op jit(solution)/shard_map/all_to_all | solution.py:62
  1612.5 89.2 %all-to-all-done.15 = f32[16,256,256]{2,0,1:T(8,128)} async-done(((f32[16,256,256]{2,0,1:T(8,128)}), f32[16,256,256]{2,0,1:T(8,128)}, u32[]{:S(2)}, u32[]{:S(2)}) %all-to-all-start.15) | async-done | bytes 4194336 | tf_op jit(solution)/shard_map/all_to_all | solution.py:63
  1717.1 5.0 all-to-all-start.17
  1722.1 6.0 fusion.175
  1736.6 79.5 %all-to-all-done.17 = f32[128,32,256]{2,1,0:T(8,128)} async-done(((f32[128,32,256]{2,1,0:T(8,128)}), f32[128,32,256]{2,1,0:T(8,128)}, u32[]{:S(2)}, u32[]{:S(2)}) %all-to-all-start.17) | async-done | bytes 4194336 | tf_op jit(solution)/shard_map/all_to_all | solution.py:68
  1816.1 97.8 %all_to_all.343 = f32[128,32,256]{2,1,0:T(8,128)S(1)} all-to-all(f32[128,32,256]{2,1,0:T(8,128)} %copy.200), channel_id=1, replica_groups=mesh['view'=4,'brick'=8] {'brick'}, dimensions={0} | all-to-all | bytes 8388608 | tf_op jit(solution)/shard_map/all_to_all | solution.py:67
  1913.9 10.6 multiply_add_fusion
  1942.9 87.1 %all-to-all-done.19 = f32[16,256,256]{2,0,1:T(8,128)} async-done(((f32[16,256,256]{2,0,1:T(8,128)}), f32[16,256,256]{2,0,1:T(8,128)}, u32[]{:S(2)}, u32[]{:S(2)}) %all-to-all-start.19) | async-done | bytes 4194336 | tf_op jit(solution)/shard_map/all_to_all | solution.py:75
  2034.8 4.9 copy.209
  2039.6 89.1 %all-to-all-done.18 = f32[16,256,256]{2,0,1:T(8,128)} async-done(((f32[16,256,256]{2,0,1:T(8,128)}), f32[16,256,256]{2,0,1:T(8,128)}, u32[]{:S(2)}, u32[]{:S(2)}) %all-to-all-start.18) | async-done | bytes 4194336 | tf_op jit(solution)/shard_map/all_to_all | solution.py:74
  2144.9 5.0 all-to-all-start.21
  2150.0 6.0 fusion.171
  2164.7 79.2 %all-to-all-done.21 = f32[128,32,256]{2,1,0:T(8,128)} async-done(((f32[128,32,256]{2,1,0:T(8,128)}), f32[128,32,256]{2,1,0:T(8,128)}, u32[]{:S(2)}, u32[]{:S(2)}) %all-to-all-start.21) | async-done | bytes 4194336 | tf_op jit(solution)/shard_map/all_to_all | solution.py:80
  2251.1 7.1 fusion.96
  2258.2 7.2 fusion.75
  2265.4 77.1 %all-to-all-done.20 = f32[128,32,256]{2,1,0:T(8,128)} async-done(((f32[128,32,256]{2,1,0:T(8,128)}), f32[128,32,256]{2,1,0:T(8,128)}, u32[]{:S(2)}, u32[]{:S(2)}) %all-to-all-start.20) | async-done | bytes 4194336 | tf_op jit(solution)/shard_map/all_to_all | solution.py:79
  2345.0 5.1 fusion.73
  2350.1 5.1 fusion.117
  2355.2 4.8 fusion
  2360.1 6.6 multiply_multiply_fusion
  2366.7 102.6 %all-reduce.4.cloned.1.call-done = f32[16,256,256]{2,1,0:T(8,128)} async-done(((f32[16,256,256]{2,1,0:T(8,128)}), f32[16,256,256]{2,1,0:T(8,128)}) %all-reduce.4.cloned.1.call-update) | async-done | bytes 4194320 | tf_op jit(solution)/shard_map/psum | solution.py:112
  2469.4 7.6 multiply_divide_fusion
  (163 shorter events, 329.1 us)
Async XLA Ops:
  7.2 1.0 copy-start
  7.2 6.6 copy-start.35
  24.3 100.4 %all-to-all-start = ((f32[16,256,256]{2,0,1:T(8,128)}), f32[16,256,256]{2,0,1:T(8,128)}, u32[]{:S(2)}, u32[]{:S(2)}) async-start(f32[16,256,256]{2,0,1:T(8,128)} %copy.144), calls=%async_computation | async-start | bytes 8388608 | tf_op jit(solution)/shard_map/all_to_all | solution.py:51
  30.6 10.8 copy-start.34
  41.3 15.7 copy-start.27
  49.0 8.1 copy-start.3
  124.7 98.6 %all-to-all-start.5 = ((f32[16,256,256]{2,0,1:T(8,128)}), f32[16,256,256]{2,0,1:T(8,128)}, u32[]{:S(2)}, u32[]{:S(2)}) async-start(f32[16,256,256]{2,0,1:T(8,128)} %copy.165), calls=%async_computation.5 | async-start | bytes 8388608 | tf_op jit(solution)/shard_map/all_to_all | solution.py:62
  129.3 4.6 copy-start.38
  223.3 98.6 %all-to-all-start.1 = ((f32[128,32,256]{2,1,0:T(8,128)}), f32[128,32,256]{2,1,0:T(8,128)}, u32[]{:S(2)}, u32[]{:S(2)}) async-start(f32[128,32,256]{2,1,0:T(8,128)} %copy.148), calls=%async_computation.1 | async-start | bytes 8388608 | tf_op jit(solution)/shard_map/all_to_all | solution.py:55
  227.8 11.0 copy-start.4
  321.8 98.6 %all-to-all-start.6 = ((f32[16,256,256]{2,0,1:T(8,128)}), f32[16,256,256]{2,0,1:T(8,128)}, u32[]{:S(2)}, u32[]{:S(2)}) async-start(f32[16,256,256]{2,0,1:T(8,128)} %copy.171), calls=%async_computation.6 | async-start | bytes 8388608 | tf_op jit(solution)/shard_map/all_to_all | solution.py:63
  326.4 182.2 %all-reduce.6.cloned.1.call-start = ((), (), s32[]{:S(2)}) async-start(), calls=%async_computation.23 | async-start | bytes 16777216 | tf_op jit(solution)/shard_map/psum | solution.py:99
  326.5 2.6 copy-start.36
  326.5 2.6 copy-start.37
  329.1 5.5 copy-start.10
  423.3 4.0 copy-start.13
  423.3 4.0 copy-start.12
  436.0 100.8 %all-to-all-start.9 = ((f32[128,32,256]{2,1,0:T(8,128)}), f32[128,32,256]{2,1,0:T(8,128)}, u32[]{:S(2)}, u32[]{:S(2)}) async-start(f32[128,32,256]{2,1,0:T(8,128)} %copy.175), calls=%async_computation.9 | async-start | bytes 8388608 | tf_op jit(solution)/shard_map/all_to_all | solution.py:68
  512.8 4.4 copy-start.2
  517.2 10.2 copy-start.5
  521.8 5.6 copy-start.28
  536.8 98.9 %all-to-all-start.2 = ((f32[16,256,256]{2,0,1:T(8,128)}), f32[16,256,256]{2,0,1:T(8,128)}, u32[]{:S(2)}, u32[]{:S(2)}) async-start(f32[16,256,256]{2,0,1:T(8,128)} %copy.152), calls=%async_computation.2 | async-start | bytes 8388608 | tf_op jit(solution)/shard_map/all_to_all | solution.py:62
  541.6 7.5 copy-start.6
  635.6 98.8 %all-to-all-start.3 = ((f32[16,256,256]{2,0,1:T(8,128)}), f32[16,256,256]{2,0,1:T(8,128)}, u32[]{:S(2)}, u32[]{:S(2)}) async-start(f32[16,256,256]{2,0,1:T(8,128)} %copy.156), calls=%async_computation.3 | async-start | bytes 8388608 | tf_op jit(solution)/shard_map/all_to_all | solution.py:63
  640.4 6.0 copy-start.14
  734.4 99.0 %all-to-all-start.7 = ((f32[128,32,256]{2,1,0:T(8,128)}), f32[128,32,256]{2,1,0:T(8,128)}, u32[]{:S(2)}, u32[]{:S(2)}) async-start(f32[128,32,256]{2,1,0:T(8,128)} %copy.173), calls=%async_computation.7 | async-start | bytes 8388608 | tf_op jit(solution)/shard_map/all_to_all | solution.py:67
  742.2 8.4 copy-start.19
  746.6 4.0 copy-start.20
  833.4 98.7 %all-to-all-start.8 = ((f32[128,32,256]{2,1,0:T(8,128)}), f32[128,32,256]{2,1,0:T(8,128)}, u32[]{:S(2)}, u32[]{:S(2)}) async-start(f32[128,32,256]{2,1,0:T(8,128)} %copy.174), calls=%async_computation.8 | async-start | bytes 8388608 | tf_op jit(solution)/shard_map/all_to_all | solution.py:68
  838.1 6.0 copy-start.21
  1047.4 98.6 %all-to-all-start.11 = ((f32[16,256,256]{2,0,1:T(8,128)}), f32[16,256,256]{2,0,1:T(8,128)}, u32[]{:S(2)}, u32[]{:S(2)}) async-start(f32[16,256,256]{2,0,1:T(8,128)} %copy.181), calls=%async_computation.11 | async-start | bytes 8388608 | tf_op jit(solution)/shard_map/all_to_all | solution.py:75
  1146.0 99.0 %all-to-all-start.10 = ((f32[16,256,256]{2,0,1:T(8,128)}), f32[16,256,256]{2,0,1:T(8,128)}, u32[]{:S(2)}, u32[]{:S(2)}) async-start(f32[16,256,256]{2,0,1:T(8,128)} %copy.177), calls=%async_computation.10 | async-start | bytes 8388608 | tf_op jit(solution)/shard_map/all_to_all | solution.py:74
  1245.0 3.4 copy-start.15
  1248.0 4.5 copy-start.25
  1261.3 98.8 %all-to-all-start.13 = ((f32[128,32,256]{2,1,0:T(8,128)}), f32[128,32,256]{2,1,0:T(8,128)}, u32[]{:S(2)}, u32[]{:S(2)}) async-start(f32[128,32,256]{2,1,0:T(8,128)} %copy.187), calls=%async_computation.13 | async-start | bytes 8388608 | tf_op jit(solution)/shard_map/all_to_all | solution.py:80
  1266.0 6.0 copy-start.16
  1360.1 98.6 %all-to-all-start.12 = ((f32[128,32,256]{2,1,0:T(8,128)}), f32[128,32,256]{2,1,0:T(8,128)}, u32[]{:S(2)}, u32[]{:S(2)}) async-start(f32[128,32,256]{2,1,0:T(8,128)} %copy.184), calls=%async_computation.12 | async-start | bytes 8388608 | tf_op jit(solution)/shard_map/all_to_all | solution.py:79
  1465.9 5.1 copy-start.32
  1471.0 4.9 copy-start.11
  1471.0 4.9 copy-start.30
  1485.3 9.6 copy-start.7
  1490.1 4.8 copy-start.29
  1504.3 98.6 %all-to-all-start.14 = ((f32[16,256,256]{2,0,1:T(8,128)}), f32[16,256,256]{2,0,1:T(8,128)}, u32[]{:S(2)}, u32[]{:S(2)}) async-start(f32[16,256,256]{2,0,1:T(8,128)} %copy.194), calls=%async_computation.14 | async-start | bytes 8388608 | tf_op jit(solution)/shard_map/all_to_all | solution.py:62
  1508.9 7.5 copy-start.8
  1602.9 98.8 %all-to-all-start.15 = ((f32[16,256,256]{2,0,1:T(8,128)}), f32[16,256,256]{2,0,1:T(8,128)}, u32[]{:S(2)}, u32[]{:S(2)}) async-start(f32[16,256,256]{2,0,1:T(8,128)} %copy.198), calls=%async_computation.15 | async-start | bytes 8388608 | tf_op jit(solution)/shard_map/all_to_all | solution.py:63
  1704.5 4.0 copy-start.23
  1704.5 4.0 copy-start.22
  1717.1 99.0 %all-to-all-start.17 = ((f32[128,32,256]{2,1,0:T(8,128)}), f32[128,32,256]{2,1,0:T(8,128)}, u32[]{:S(2)}, u32[]{:S(2)}) async-start(f32[128,32,256]{2,1,0:T(8,128)} %copy.201), calls=%async_computation.17 | async-start | bytes 8388608 | tf_op jit(solution)/shard_map/all_to_all | solution.py:68
  1722.1 6.0 copy-start.24
  1931.4 98.6 %all-to-all-start.19 = ((f32[16,256,256]{2,0,1:T(8,128)}), f32[16,256,256]{2,0,1:T(8,128)}, u32[]{:S(2)}, u32[]{:S(2)}) async-start(f32[16,256,256]{2,0,1:T(8,128)} %copy.207), calls=%async_computation.19 | async-start | bytes 8388608 | tf_op jit(solution)/shard_map/all_to_all | solution.py:75
  2030.0 98.8 %all-to-all-start.18 = ((f32[16,256,256]{2,0,1:T(8,128)}), f32[16,256,256]{2,0,1:T(8,128)}, u32[]{:S(2)}, u32[]{:S(2)}) async-start(f32[16,256,256]{2,0,1:T(8,128)} %copy.203), calls=%async_computation.18 | async-start | bytes 8388608 | tf_op jit(solution)/shard_map/all_to_all | solution.py:74
  2128.8 3.4 copy-start.17
  2131.8 4.5 copy-start.26
  2144.9 99.0 %all-to-all-start.21 = ((f32[128,32,256]{2,1,0:T(8,128)}), f32[128,32,256]{2,1,0:T(8,128)}, u32[]{:S(2)}, u32[]{:S(2)}) async-start(f32[128,32,256]{2,1,0:T(8,128)} %copy.213), calls=%async_computation.21 | async-start | bytes 8388608 | tf_op jit(solution)/shard_map/all_to_all | solution.py:80
  2149.9 6.0 copy-start.18
  2243.9 98.6 %all-to-all-start.20 = ((f32[128,32,256]{2,1,0:T(8,128)}), f32[128,32,256]{2,1,0:T(8,128)}, u32[]{:S(2)}, u32[]{:S(2)}) async-start(f32[128,32,256]{2,1,0:T(8,128)} %copy.210), calls=%async_computation.20 | async-start | bytes 8388608 | tf_op jit(solution)/shard_map/all_to_all | solution.py:79
  2248.5 220.8 %all-reduce.4.cloned.1.call-start = ((), (), s32[]{:S(2)}) async-start(), calls=%async_computation.22 | async-start | bytes 8388608 | tf_op jit(solution)/shard_map/psum | solution.py:112
  2350.1 5.1 copy-start.33
  2355.2 4.9 copy-start.9
  2355.2 4.9 copy-start.31
  2469.4 7.6 copy-start.1
Sparse Core Ops, SparseCore 0:
  334.7 173.9 all-reduce.5
  2366.9 102.4 all-reduce.3
where the time goes:
time: 2490 us; the launch traced here: 2480 us
  waiting for transfers between devices  1670 us (67%)
  matrix products  297 us (12%)
  blocking collectives  196 us (8%)
  local copies, waits for them, and re-layouts  168 us (7%)
  starting transfers between devices  96 us (4%)
  other arithmetic  38.3 us (2%)
    dot_general x50, matrix products, along_axis(): jnp.einsum(einsum_forms[axis_index], values_in, table, precision=highest)  277 us
    all_to_all x3, waiting for transfers between devices, forward_transform(): lax.all_to_all(imag_part, 'brick', split_axis=1, concat_axis=0, tiled=True)  250 us
    all_to_all x3, waiting for transfers between devices, forward_transform(): lax.all_to_all(real_part, 'brick', split_axis=1, concat_axis=0, tiled=True)  229 us
    all_to_all x2, blocking collectives, forward_transform(): lax.all_to_all(depth_real, 'brick', split_axis=0, concat_axis=1, tiled=True)  196 us
    all_to_all x2, waiting for transfers between devices, inverse_transform(): lax.all_to_all(real_part, 'brick', split_axis=1, concat_axis=0, tiled=True)  178 us
    all_to_all x2, waiting for transfers between devices, inverse_transform(): lax.all_to_all(imag_part, 'brick', split_axis=1, concat_axis=0, tiled=True)  174 us
    all_to_all x3, waiting for transfers between devices, forward_transform(): lax.all_to_all(depth_imag, 'brick', split_axis=0, concat_axis=1, tiled=True)  159 us
    all_to_all x2, waiting for transfers between devices, inverse_transform(): lax.all_to_all(imag_part, 'brick', split_axis=0, concat_axis=1, tiled=True)  158 us
  transfers between devices with their start and end apart: 22, of which 21 were waited for; matrix products, arithmetic and copies ran while one was open for 13% of the time, Pallas kernels for 0%

commit v1 on v0

--- a/solution.py
+++ b/solution.py
@@ -65,7 +65,12 @@
     )
     return (
         lax.all_to_all(depth_real, "brick", split_axis=0, concat_axis=1, tiled=True),
-        lax.all_to_all(depth_imag, "brick", split_axis=0, concat_axis=1, tiled=True),
+        jnp.concatenate(
+            lax.all_to_all(
+                jnp.stack(jnp.split(depth_imag, lax.axis_size("brick"), 0), axis=0), "brick", 0, 0
+            ),
+            1,
+        ),
     )
 
 

time: 2490 us -> 2480 us (level)
  blocking collectives: 196 us -> 390 us
  waiting for transfers between devices: 1670 us -> 1490 us
    all_to_all x5 -> x1, waiting for transfers between devices: 333 us -> 74.3 us  [forward_transform(): lax.all_to_all(jnp.stack(jnp.split(depth_imag, lax.axis_size('brick'), 0)...]
    all_to_all x2 -> x4, blocking collectives: 196 us -> 390 us  [the longest x2 195 us: forward_transform(): lax.all_to_all(jnp.stack(jnp.split(depth_imag, lax.axis_size('brick'), 0)...]
    all_to_all x1 -> x3, waiting for transfers between devices: 74.3 us -> 154 us  [forward_transform(): lax.all_to_all(depth_real, 'brick', split_axis=0, concat_axis=1, tiled=True)]
  transfers between devices with their start and end apart: 22 -> 20, of which waited for: 21 -> 19; matrix products, arithmetic and copies ran while one was open for 13% -> 13% of each run, Pallas kernels for 0% -> 0%
where the time goes in v1:
time: 2480 us; the launch traced here: 2470 us
  waiting for transfers between devices  1490 us (60%)
  blocking collectives  390 us (16%)
  matrix products  297 us (12%)
  local copies, waits for them, and re-layouts  149 us (6%)
  starting transfers between devices  86.9 us (4%)
  other arithmetic  43.1 us (2%)
    dot_general x50, matrix products, along_axis(): jnp.einsum(einsum_forms[axis_index], values_in, table, precision=highest)  277 us
    all_to_all x3, waiting for transfers between devices, forward_transform(): lax.all_to_all(imag_part, 'brick', split_axis=1, concat_axis=0, tiled=True)  247 us
    all_to_all x3, waiting for transfers between devices, forward_transform(): lax.all_to_all(real_part, 'brick', split_axis=1, concat_axis=0, tiled=True)  229 us
    all_to_all x2, blocking collectives, forward_transform(): lax.all_to_all(jnp.stack(jnp.split(depth_imag, lax.axis_size('brick'), 0)...  195 us
    all_to_all x2, blocking collectives, inverse_transform(): lax.all_to_all(imag_part, 'brick', split_axis=1, concat_axis=0, tiled=True)  195 us
    all_to_all x2, waiting for transfers between devices, inverse_transform(): lax.all_to_all(real_part, 'brick', split_axis=1, concat_axis=0, tiled=True)  178 us
    all_to_all x2, waiting for transfers between devices, inverse_transform(): lax.all_to_all(imag_part, 'brick', split_axis=0, concat_axis=1, tiled=True)  158 us
    all_to_all x3, waiting for transfers between devices, forward_transform(): lax.all_to_all(depth_real, 'brick', split_axis=0, concat_axis=1, tiled=True)  154 us
  transfers between devices with their start and end apart: 20, of which 19 were waited for; matrix products, arithmetic and copies ran while one was open for 13% of the time, Pallas kernels for 0%

profile of v1, /device:TPU:0, one launch (start us, length us, event | category | flops | bytes accessed | tf_op | source)
XLA Modules:
  0.0 2472.5 jit_solution(1218659012885809513)
XLA Ops:
  8.1 5.7 fusion.25
  13.8 5.0 convolution_bitcast_fusion
  18.8 5.4 copy.150
  24.3 6.3 all-to-all-start
  30.6 10.7 fusion.16
  41.3 7.6 fusion.18
  48.9 8.1 fusion.10
  57.0 7.6 add_bitcast_fusion.1
  69.3 55.4 %all-to-all-done = f32[16,256,256]{2,0,1:T(8,128)} async-done(((f32[16,256,256]{2,0,1:T(8,128)}), f32[16,256,256]{2,0,1:T(8,128)}, u32[]{:S(2)}, u32[]{:S(2)}) %all-to-all-start) | async-done | bytes 4194336 | tf_op jit(solution)/shard_map/all_to_all | solution.py:51
  133.9 9.4 fusion.47
  143.3 5.4 copy.154
  148.7 74.5 %all-to-all-done.5 = f32[16,256,256]{2,0,1:T(8,128)} async-done(((f32[16,256,256]{2,0,1:T(8,128)}), f32[16,256,256]{2,0,1:T(8,128)}, u32[]{:S(2)}, u32[]{:S(2)}) %all-to-all-start.5) | async-done | bytes 4194336 | tf_op jit(solution)/shard_map/all_to_all | solution.py:62
  227.9 11.0 fusion.8
  238.9 7.6 subtract_bitcast_fusion.1
  250.9 70.9 %all-to-all-done.1 = f32[128,32,256]{2,1,0:T(8,128)} async-done(((f32[128,32,256]{2,1,0:T(8,128)}), f32[128,32,256]{2,1,0:T(8,128)}, u32[]{:S(2)}, u32[]{:S(2)}) %all-to-all-start.1) | async-done | bytes 4194336 | tf_op jit(solution)/shard_map/all_to_all | solution.py:55
  329.1 5.5 fusion.24
  334.6 4.9 copy.172
  339.5 80.9 %all-to-all-done.6 = f32[16,256,256]{2,0,1:T(8,128)} async-done(((f32[16,256,256]{2,0,1:T(8,128)}), f32[16,256,256]{2,0,1:T(8,128)}, u32[]{:S(2)}, u32[]{:S(2)}) %all-to-all-start.6) | async-done | bytes 4194336 | tf_op jit(solution)/shard_map/all_to_all | solution.py:63
  441.3 67.4 %all-reduce.6.cloned.1.call-done = (f32[16,256,256]{2,1,0:T(8,128)}, f32[16,256,256]{2,1,0:T(8,128)}) async-done(((f32[16,256,256]{2,1,0:T(8,128)}, f32[16,256,256]{2,1,0:T(8,128)}), (f32[16,256,256]{2,1,0:T(8,128)}, f32[16,256,256]{2,1,0:T(8,128)})) %all-reduce.6.cloned.1.call-update) | async-done | bytes 8388624 | tf_op jit(solution)/shard_map/psum | solution.py:104
  521.9 5.6 fusion.135
  527.4 4.9 add_bitcast_fusion.2
  541.6 7.5 fusion.111
  558.3 77.3 %all-to-all-done.2 = f32[16,256,256]{2,0,1:T(8,128)} async-done(((f32[16,256,256]{2,0,1:T(8,128)}), f32[16,256,256]{2,0,1:T(8,128)}, u32[]{:S(2)}, u32[]{:S(2)}) %all-to-all-start.2) | async-done | bytes 4194336 | tf_op jit(solution)/shard_map/all_to_all | solution.py:62
  640.5 6.0 fusion.205
  657.4 77.1 %all-to-all-done.3 = f32[16,256,256]{2,0,1:T(8,128)} async-done(((f32[16,256,256]{2,0,1:T(8,128)}), f32[16,256,256]{2,0,1:T(8,128)}, u32[]{:S(2)}, u32[]{:S(2)}) %all-to-all-start.3) | async-done | bytes 4194336 | tf_op jit(solution)/shard_map/all_to_all | solution.py:63
  734.4 5.0 all-to-all-start.9
  759.1 74.3 %all-to-all-done.9 = f32[8,16,32,256]{3,1,2,0:T(8,128)} async-done(((f32[8,16,32,256]{3,1,2,0:T(8,128)}), f32[8,16,32,256]{3,1,2,0:T(8,128)}, u32[]{:S(2)}, u32[]{:S(2)}) %all-to-all-start.9) | async-done | bytes 4194336 | tf_op jit(solution)/shard_map/all_to_all | solution.py:69
  838.2 6.0 fusion.207
  855.1 77.1 %all-to-all-done.4 = f32[128,32,256]{2,1,0:T(8,128)} async-done(((f32[128,32,256]{2,1,0:T(8,128)}), f32[128,32,256]{2,1,0:T(8,128)}, u32[]{:S(2)}, u32[]{:S(2)}) %all-to-all-start.4) | async-done | bytes 4194336 | tf_op jit(solution)/shard_map/all_to_all | solution.py:67
  932.2 97.6 %all_to_all.339 = f32[8,16,32,256]{3,1,2,0:T(8,128)S(1)} all-to-all(f32[8,16,32,256]{3,1,2,0:T(8,128)} %fusion.86), channel_id=1, replica_groups=mesh['view'=4,'brick'=8] {'brick'}, dimensions={0} | all-to-all | bytes 8388608 | tf_op jit(solution)/shard_map/all_to_all | solution.py:69
  1029.8 13.0 multiply_subtract_fusion.1
  1042.8 97.3 %all_to_all.340 = f32[16,256,256]{2,0,1:T(8,128)} all-to-all(f32[16,256,256]{2,0,1:T(8,128)S(1)} %bitcast.455), channel_id=1, replica_groups=mesh['view'=4,'brick'=8] {'brick'}, dimensions={1} | all-to-all | bytes 8388608 | tf_op jit(solution)/shard_map/all_to_all | solution.py:80
  1140.1 5.0 all-to-all-start.10
  1149.9 89.2 %all-to-all-done.10 = f32[16,256,256]{2,0,1:T(8,128)} async-done(((f32[16,256,256]{2,0,1:T(8,128)}), f32[16,256,256]{2,0,1:T(8,128)}, u32[]{:S(2)}, u32[]{:S(2)}) %all-to-all-start.10) | async-done | bytes 4194336 | tf_op jit(solution)/shard_map/all_to_all | solution.py:79
  1260.2 6.0 fusion.203
  1274.9 79.3 %all-to-all-done.13 = f32[128,32,256]{2,1,0:T(8,128)} async-done(((f32[128,32,256]{2,1,0:T(8,128)}), f32[128,32,256]{2,1,0:T(8,128)}, u32[]{:S(2)}, u32[]{:S(2)}) %all-to-all-start.13) | async-done | bytes 4194336 | tf_op jit(solution)/shard_map/all_to_all | solution.py:85
  1361.2 7.1 fusion.123
  1368.3 7.5 fusion.106
  1375.8 76.9 %all-to-all-done.12 = f32[128,32,256]{2,1,0:T(8,128)} async-done(((f32[128,32,256]{2,1,0:T(8,128)}), f32[128,32,256]{2,1,0:T(8,128)}, u32[]{:S(2)}, u32[]{:S(2)}) %all-to-all-start.12) | async-done | bytes 4194336 | tf_op jit(solution)/shard_map/all_to_all | solution.py:84
  1460.0 5.1 fusion.137
  1470.0 5.0 bitcast_divide_fusion
  1503.0 7.5 fusion.101
  1519.5 77.4 %all-to-all-done.14 = f32[16,256,256]{2,0,1:T(8,128)} async-done(((f32[16,256,256]{2,0,1:T(8,128)}), f32[16,256,256]{2,0,1:T(8,128)}, u32[]{:S(2)}, u32[]{:S(2)}) %all-to-all-start.14) | async-done | bytes 4194336 | tf_op jit(solution)/shard_map/all_to_all | solution.py:62
  1601.7 4.8 copy.197
  1606.6 89.2 %all-to-all-done.15 = f32[16,256,256]{2,0,1:T(8,128)} async-done(((f32[16,256,256]{2,0,1:T(8,128)}), f32[16,256,256]{2,0,1:T(8,128)}, u32[]{:S(2)}, u32[]{:S(2)}) %all-to-all-start.15) | async-done | bytes 4194336 | tf_op jit(solution)/shard_map/all_to_all | solution.py:63
  1711.7 5.0 all-to-all-start.16
  1716.6 6.0 fusion.197
  1733.6 77.0 %all-to-all-done.16 = f32[128,32,256]{2,1,0:T(8,128)} async-done(((f32[128,32,256]{2,1,0:T(8,128)}), f32[128,32,256]{2,1,0:T(8,128)}, u32[]{:S(2)}, u32[]{:S(2)}) %all-to-all-start.16) | async-done | bytes 4194336 | tf_op jit(solution)/shard_map/all_to_all | solution.py:67
  1810.6 97.6 %all_to_all.341 = f32[8,16,32,256]{3,1,2,0:T(8,128)S(1)} all-to-all(f32[8,16,32,256]{3,1,2,0:T(8,128)} %fusion.70), channel_id=1, replica_groups=mesh['view'=4,'brick'=8] {'brick'}, dimensions={0} | all-to-all | bytes 8388608 | tf_op jit(solution)/shard_map/all_to_all | solution.py:69
  1908.3 13.0 multiply_add_fusion
  1921.2 97.3 %all_to_all.342 = f32[16,256,256]{2,0,1:T(8,128)} all-to-all(f32[16,256,256]{2,0,1:T(8,128)S(1)} %bitcast.454), channel_id=1, replica_groups=mesh['view'=4,'brick'=8] {'brick'}, dimensions={1} | all-to-all | bytes 8388608 | tf_op jit(solution)/shard_map/all_to_all | solution.py:80
  2023.3 4.8 copy.208
  2028.1 89.2 %all-to-all-done.18 = f32[16,256,256]{2,0,1:T(8,128)} async-done(((f32[16,256,256]{2,0,1:T(8,128)}), f32[16,256,256]{2,0,1:T(8,128)}, u32[]{:S(2)}, u32[]{:S(2)}) %all-to-all-start.18) | async-done | bytes 4194336 | tf_op jit(solution)/shard_map/all_to_all | solution.py:79
  2133.4 5.0 all-to-all-start.21
  2138.4 6.0 fusion.195
  2153.2 79.2 %all-to-all-done.21 = f32[128,32,256]{2,1,0:T(8,128)} async-done(((f32[128,32,256]{2,1,0:T(8,128)}), f32[128,32,256]{2,1,0:T(8,128)}, u32[]{:S(2)}, u32[]{:S(2)}) %all-to-all-start.21) | async-done | bytes 4194336 | tf_op jit(solution)/shard_map/all_to_all | solution.py:85
  2239.5 7.1 fusion.120
  2246.7 7.2 fusion.99
  2253.9 77.1 %all-to-all-done.20 = f32[128,32,256]{2,1,0:T(8,128)} async-done(((f32[128,32,256]{2,1,0:T(8,128)}), f32[128,32,256]{2,1,0:T(8,128)}, u32[]{:S(2)}, u32[]{:S(2)}) %all-to-all-start.20) | async-done | bytes 4194336 | tf_op jit(solution)/shard_map/all_to_all | solution.py:84
  2333.5 5.1 fusion.97
  2338.6 5.1 fusion.141
  2348.6 6.6 multiply_multiply_fusion
  2355.2 102.6 %all-reduce.4.cloned.1.call-done = f32[16,256,256]{2,1,0:T(8,128)} async-done(((f32[16,256,256]{2,1,0:T(8,128)}), f32[16,256,256]{2,1,0:T(8,128)}) %all-reduce.4.cloned.1.call-update) | async-done | bytes 4194320 | tf_op jit(solution)/shard_map/psum | solution.py:117
  2457.8 7.6 multiply_divide_fusion
  (174 shorter events, 300.6 us)
Async XLA Ops:
  7.2 1.0 copy-start
  7.2 6.6 copy-start.35
  24.3 100.4 %all-to-all-start = ((f32[16,256,256]{2,0,1:T(8,128)}), f32[16,256,256]{2,0,1:T(8,128)}, u32[]{:S(2)}, u32[]{:S(2)}) async-start(f32[16,256,256]{2,0,1:T(8,128)} %copy.150), calls=%async_computation | async-start | bytes 8388608 | tf_op jit(solution)/shard_map/all_to_all | solution.py:51
  30.6 10.7 copy-start.34
  41.3 15.7 copy-start.27
  48.9 8.1 copy-start.3
  124.7 98.6 %all-to-all-start.5 = ((f32[16,256,256]{2,0,1:T(8,128)}), f32[16,256,256]{2,0,1:T(8,128)}, u32[]{:S(2)}, u32[]{:S(2)}) async-start(f32[16,256,256]{2,0,1:T(8,128)} %copy.171), calls=%async_computation.5 | async-start | bytes 8388608 | tf_op jit(solution)/shard_map/all_to_all | solution.py:62
  129.3 4.6 copy-start.38
  223.3 98.6 %all-to-all-start.1 = ((f32[128,32,256]{2,1,0:T(8,128)}), f32[128,32,256]{2,1,0:T(8,128)}, u32[]{:S(2)}, u32[]{:S(2)}) async-start(f32[128,32,256]{2,1,0:T(8,128)} %copy.154), calls=%async_computation.1 | async-start | bytes 8388608 | tf_op jit(solution)/shard_map/all_to_all | solution.py:55
  227.8 11.0 copy-start.4
  321.9 98.6 %all-to-all-start.6 = ((f32[16,256,256]{2,0,1:T(8,128)}), f32[16,256,256]{2,0,1:T(8,128)}, u32[]{:S(2)}, u32[]{:S(2)}) async-start(f32[16,256,256]{2,0,1:T(8,128)} %copy.177), calls=%async_computation.6 | async-start | bytes 8388608 | tf_op jit(solution)/shard_map/all_to_all | solution.py:63
  326.4 182.2 %all-reduce.6.cloned.1.call-start = ((), (), s32[]{:S(2)}) async-start(), calls=%async_computation.23 | async-start | bytes 16777216 | tf_op jit(solution)/shard_map/psum | solution.py:104
  326.5 2.6 copy-start.36
  326.5 2.6 copy-start.37
  329.1 5.5 copy-start.10
  420.4 3.5 copy-start.12
  423.5 4.5 copy-start.14
  436.7 100.1 %all-to-all-start.7 = ((f32[128,32,256]{2,1,0:T(8,128)}), f32[128,32,256]{2,1,0:T(8,128)}, u32[]{:S(2)}, u32[]{:S(2)}) async-start(f32[128,32,256]{2,1,0:T(8,128)} %copy.179), calls=%async_computation.7 | async-start | bytes 8388608 | tf_op jit(solution)/shard_map/all_to_all | solution.py:67
  512.8 4.4 copy-start.2
  517.2 10.2 copy-start.5
  521.8 5.6 copy-start.28
  536.8 98.9 %all-to-all-start.2 = ((f32[16,256,256]{2,0,1:T(8,128)}), f32[16,256,256]{2,0,1:T(8,128)}, u32[]{:S(2)}, u32[]{:S(2)}) async-start(f32[16,256,256]{2,0,1:T(8,128)} %copy.158), calls=%async_computation.2 | async-start | bytes 8388608 | tf_op jit(solution)/shard_map/all_to_all | solution.py:62
  541.6 7.5 copy-start.6
  635.6 98.8 %all-to-all-start.3 = ((f32[16,256,256]{2,0,1:T(8,128)}), f32[16,256,256]{2,0,1:T(8,128)}, u32[]{:S(2)}, u32[]{:S(2)}) async-start(f32[16,256,256]{2,0,1:T(8,128)} %copy.162), calls=%async_computation.3 | async-start | bytes 8388608 | tf_op jit(solution)/shard_map/all_to_all | solution.py:63
  640.4 6.0 copy-start.13
  734.4 99.0 %all-to-all-start.9 = ((f32[8,16,32,256]{3,1,2,0:T(8,128)}), f32[8,16,32,256]{3,1,2,0:T(8,128)}, u32[]{:S(2)}, u32[]{:S(2)}) async-start(f32[8,16,32,256]{3,1,2,0:T(8,128)} %fusion.78), calls=%async_computation.9 | async-start | bytes 8388608 | tf_op jit(solution)/shard_map/all_to_all | solution.py:69
  742.2 4.4 copy-start.15
  746.6 4.0 copy-start.23
  833.4 98.8 %all-to-all-start.4 = ((f32[128,32,256]{2,1,0:T(8,128)}), f32[128,32,256]{2,1,0:T(8,128)}, u32[]{:S(2)}, u32[]{:S(2)}) async-start(f32[128,32,256]{2,1,0:T(8,128)} %copy.164), calls=%async_computation.4 | async-start | bytes 8388608 | tf_op jit(solution)/shard_map/all_to_all | solution.py:67
  838.2 6.0 copy-start.16
  1140.1 99.0 %all-to-all-start.10 = ((f32[16,256,256]{2,0,1:T(8,128)}), f32[16,256,256]{2,0,1:T(8,128)}, u32[]{:S(2)}, u32[]{:S(2)}) async-start(f32[16,256,256]{2,0,1:T(8,128)} %bitcast.453), calls=%async_computation.10 | async-start | bytes 8388608 | tf_op jit(solution)/shard_map/all_to_all | solution.py:79
  1239.1 3.4 copy-start.17
  1242.1 4.5 copy-start.24
  1255.4 98.8 %all-to-all-start.13 = ((f32[128,32,256]{2,1,0:T(8,128)}), f32[128,32,256]{2,1,0:T(8,128)}, u32[]{:S(2)}, u32[]{:S(2)}) async-start(f32[128,32,256]{2,1,0:T(8,128)} %copy.189), calls=%async_computation.13 | async-start | bytes 8388608 | tf_op jit(solution)/shard_map/all_to_all | solution.py:85
  1260.1 6.0 copy-start.18
  1354.1 98.6 %all-to-all-start.12 = ((f32[128,32,256]{2,1,0:T(8,128)}), f32[128,32,256]{2,1,0:T(8,128)}, u32[]{:S(2)}, u32[]{:S(2)}) async-start(f32[128,32,256]{2,1,0:T(8,128)} %copy.186), calls=%async_computation.12 | async-start | bytes 8388608 | tf_op jit(solution)/shard_map/all_to_all | solution.py:84
  1460.0 5.1 copy-start.32
  1465.1 4.9 copy-start.11
  1465.1 4.9 copy-start.30
  1479.4 9.6 copy-start.7
  1484.3 4.8 copy-start.29
  1498.4 98.6 %all-to-all-start.14 = ((f32[16,256,256]{2,0,1:T(8,128)}), f32[16,256,256]{2,0,1:T(8,128)}, u32[]{:S(2)}, u32[]{:S(2)}) async-start(f32[16,256,256]{2,0,1:T(8,128)} %copy.196), calls=%async_computation.14 | async-start | bytes 8388608 | tf_op jit(solution)/shard_map/all_to_all | solution.py:62
  1502.9 7.5 copy-start.8
  1597.0 98.8 %all-to-all-start.15 = ((f32[16,256,256]{2,0,1:T(8,128)}), f32[16,256,256]{2,0,1:T(8,128)}, u32[]{:S(2)}, u32[]{:S(2)}) async-start(f32[16,256,256]{2,0,1:T(8,128)} %copy.200), calls=%async_computation.15 | async-start | bytes 8388608 | tf_op jit(solution)/shard_map/all_to_all | solution.py:63
  1695.7 3.4 copy-start.19
  1698.7 4.5 copy-start.25
  1711.7 99.0 %all-to-all-start.16 = ((f32[128,32,256]{2,1,0:T(8,128)}), f32[128,32,256]{2,1,0:T(8,128)}, u32[]{:S(2)}, u32[]{:S(2)}) async-start(f32[128,32,256]{2,1,0:T(8,128)} %copy.202), calls=%async_computation.16 | async-start | bytes 8388608 | tf_op jit(solution)/shard_map/all_to_all | solution.py:67
  1716.6 6.0 copy-start.20
  2018.5 98.7 %all-to-all-start.18 = ((f32[16,256,256]{2,0,1:T(8,128)}), f32[16,256,256]{2,0,1:T(8,128)}, u32[]{:S(2)}, u32[]{:S(2)}) async-start(f32[16,256,256]{2,0,1:T(8,128)} %bitcast.452), calls=%async_computation.18 | async-start | bytes 8388608 | tf_op jit(solution)/shard_map/all_to_all | solution.py:79
  2117.3 3.4 copy-start.21
  2120.3 4.5 copy-start.26
  2133.4 99.0 %all-to-all-start.21 = ((f32[128,32,256]{2,1,0:T(8,128)}), f32[128,32,256]{2,1,0:T(8,128)}, u32[]{:S(2)}, u32[]{:S(2)}) async-start(f32[128,32,256]{2,1,0:T(8,128)} %copy.212), calls=%async_computation.21 | async-start | bytes 8388608 | tf_op jit(solution)/shard_map/all_to_all | solution.py:85
  2138.4 6.0 copy-start.22
  2232.4 98.6 %all-to-all-start.20 = ((f32[128,32,256]{2,1,0:T(8,128)}), f32[128,32,256]{2,1,0:T(8,128)}, u32[]{:S(2)}, u32[]{:S(2)}) async-start(f32[128,32,256]{2,1,0:T(8,128)} %copy.209), calls=%async_computation.20 | async-start | bytes 8388608 | tf_op jit(solution)/shard_map/all_to_all | solution.py:84
  2237.0 220.9 %all-reduce.4.cloned.1.call-start = ((), (), s32[]{:S(2)}) async-start(), calls=%async_computation.22 | async-start | bytes 8388608 | tf_op jit(solution)/shard_map/psum | solution.py:117
  2338.6 5.1 copy-start.33
  2343.7 4.9 copy-start.9
  2343.7 4.9 copy-start.31
  2457.8 7.6 copy-start.1
Sparse Core Ops, SparseCore 0:
  334.7 173.9 all-reduce.5
  2355.3 102.4 all-reduce.3
